TPU v7x, 512 devices: a whole 4x4x16 slice. The times are simulated.
512 devices in a mesh: dp: 16 (over z), head: 8 (over x, core), srv: 4 (over y).
Axes of the slice: x: 4, y: 4, z: 16, core: 2. Of those that a mesh axis runs over, the one named last changes fastest.
Arguments:
- queries: bfloat16 [2048, 8, 1024], P('dp', 'srv', 'head'), may hold values from -5 to 5
- keys: bfloat16 [10240, 1024], P(('dp', 'head')), may hold values from -5 to 5
- values: bfloat16 [10240, 1024], P(('dp', 'head')), may hold values from -6 to 6
- output_gradient: bfloat16 [2048, 8, 1024], P('dp', 'srv', 'head'), may hold values from -6 to 6
- doc_ids: int32 [10240], P('dp'), may hold values from 0 to 7, never falling along the last dimension, each value on 1 to 5120 neighbouring positions
Outputs:
- attention: bfloat16 [2048, 8, 1024], P('dp', 'srv', 'head')
- q_grad: bfloat16 [2048, 8, 1024], P('dp', 'srv', 'head')
- k_grad: bfloat16 [10240, 1024], P(('dp', 'head', 'srv'))
- v_grad: bfloat16 [10240, 1024], P(('dp', 'head', 'srv'))
Inputs may be any that keep to these rules, and one draw needn't show every extreme that they name: `doc_ids`: document numbers never fall along the keys; every document holds at most 5120 keys, and one holds exactly 5120.
All inputs are finite; a program needn't handle non-finite values.
Results may differ from a plain program's by a relative error of at most 0.039.
Values may be sent and summed in bfloat16 or wider, within the bound.
No kernel may reach another device: no remote copies, remote signals or barrier semaphores. Data moves between devices by JAX's collectives and lax.ppermute only.
A program may use at most 64 MiB of HBM per device.

v0:
```python
import math
import jax
import jax.numpy as jnp
from jax import lax
from jax.sharding import PartitionSpec as P

HEAD_SIZE = 128
NEGATIVE = -1e30


def local(queries, keys, values, output_gradient, doc_ids):
    home_rows, pair_heads, group_width = queries.shape
    groups = group_width // HEAD_SIZE
    scale_factor = HEAD_SIZE ** (-0.5)
    key_rows, value_rows = (
        lax.all_to_all(keys, "head", split_axis=1, concat_axis=0, tiled=True),
        lax.all_to_all(values, "head", split_axis=1, concat_axis=0, tiled=True),
    )
    key_count = key_rows.shape[0]
    servers = lax.axis_size("dp")
    server = lax.axis_index("dp")
    key_at = server * key_count + jnp.arange(key_count, dtype=jnp.int32)
    all_docs = lax.all_gather(doc_ids, "dp", axis=0, tiled=True)
    query_total = home_rows * servers
    context = all_docs.shape[0] - query_total
    query_docs = all_docs[context:]
    query_places = context + jnp.arange(query_total, dtype=jnp.int32)
    all_q, all_dout = (
        lax.all_gather(queries, "dp", axis=0, tiled=True),
        lax.all_gather(output_gradient, "dp", axis=0, tiled=True),
    )
    block_rows = math.gcd(512, query_total)
    block_count = query_total // block_rows
    key_heads = key_rows.reshape(key_count, groups, HEAD_SIZE)
    value_heads = value_rows.reshape(key_count, groups, HEAD_SIZE)
    query_blocks = all_q.reshape(block_count, block_rows, pair_heads, groups, HEAD_SIZE)
    grad_blocks = all_dout.reshape(block_count, block_rows, pair_heads, groups, HEAD_SIZE)
    place_blocks = query_places.reshape(block_count, block_rows)
    doc_blocks = query_docs.reshape(block_count, block_rows)

    def admissible(places, query_doc):
        return (key_at[None, :] <= places[:, None]) & (doc_ids[None, :] == query_doc[:, None])

    def scores_of(query_block):
        return (
            jnp.einsum("pjgd,kgd->gjpk", query_block, key_heads, preferred_element_type=jnp.float32)
            * scale_factor
        )

    def block_max(inputs):
        query_block, places, query_doc = inputs
        allowed = admissible(places, query_doc)

        def compute():
            raw_scores = scores_of(query_block)
            masked = jnp.where(allowed[None, None], raw_scores, NEGATIVE)
            return (jnp.max(masked, axis=-1).transpose(2, 1, 0), raw_scores)

        return compute()

    def block_top(inputs):
        return block_max(inputs)[0]

    local_max = lax.map(block_top, (query_blocks, place_blocks, doc_blocks))
    row_max = lax.pmax(local_max.reshape(query_total, pair_heads, groups), "dp")
    max_blocks = row_max.reshape(block_count, block_rows, pair_heads, groups)

    def block_sum(inputs):
        stored, places, query_doc, row_top = inputs
        allowed = admissible(places, query_doc)

        def compute():
            block_scores = scores_of(stored)
            shifted = block_scores - row_top.transpose(2, 1, 0)[..., None]
            weights = jnp.where(allowed[None, None], jnp.exp(shifted), 0.0)
            weighted = jnp.einsum(
                "gjpk,kgd->pjgd",
                weights.astype(jnp.bfloat16),
                value_heads,
                preferred_element_type=jnp.float32,
            )
            return (
                weighted.reshape(block_rows, pair_heads, group_width),
                jnp.sum(weights, axis=-1).transpose(2, 1, 0),
            )

        return compute()

    part_out, part_norm = lax.map(block_sum, (query_blocks, place_blocks, doc_blocks, max_blocks))
    part_out = part_out.reshape(query_total, pair_heads, group_width)
    part_norm = part_norm.reshape(query_total, pair_heads, groups)
    home_out, home_norm = (
        lax.psum_scatter(part_out, "dp", scatter_dimension=0, tiled=True),
        lax.psum_scatter(part_norm, "dp", scatter_dimension=0, tiled=True),
    )
    home_max = lax.dynamic_slice_in_dim(row_max, server * home_rows, home_rows, 0)
    attn_home = (
        home_out.reshape(home_rows, pair_heads, groups, HEAD_SIZE) / home_norm[..., None]
    ).astype(jnp.bfloat16)
    log_home = home_max + jnp.log(home_norm)
    grad_home = output_gradient.reshape(home_rows, pair_heads, groups, HEAD_SIZE).astype(
        jnp.float32
    )
    delta_home = jnp.sum(grad_home * attn_home.astype(jnp.float32), axis=-1)
    log_all, delta_all = (
        lax.all_gather(log_home, "dp", axis=0, tiled=True),
        lax.all_gather(delta_home, "dp", axis=0, tiled=True),
    )
    attention = attn_home.reshape(home_rows, pair_heads, group_width)
    log_blocks = log_all.reshape(block_count, block_rows, pair_heads, groups)
    delta_blocks = delta_all.reshape(block_count, block_rows, pair_heads, groups)

    def block_grad(totals, inputs):
        query_block, grad_block, places, query_doc, log_norm, row_delta = inputs
        allowed = admissible(places, query_doc)

        def compute():
            shifted = scores_of(query_block) - log_norm.transpose(2, 1, 0)[..., None]
            probs = jnp.where(allowed[None, None], jnp.exp(shifted), 0.0)
            value_grad = jnp.einsum(
                "gjpk,pjgd->kgd",
                probs.astype(jnp.bfloat16),
                grad_block,
                preferred_element_type=jnp.float32,
            )
            weight_grad = jnp.einsum(
                "pjgd,kgd->gjpk", grad_block, value_heads, preferred_element_type=jnp.float32
            )
            score_grad = (probs * (weight_grad - row_delta.transpose(2, 1, 0)[..., None])).astype(
                jnp.bfloat16
            )
            query_grad = (
                jnp.einsum(
                    "gjpk,kgd->pjgd", score_grad, key_heads, preferred_element_type=jnp.float32
                )
                * scale_factor
            )
            key_grad = (
                jnp.einsum(
                    "gjpk,pjgd->kgd", score_grad, query_block, preferred_element_type=jnp.float32
                )
                * scale_factor
            )
            return (query_grad.reshape(block_rows, pair_heads, group_width), key_grad, value_grad)

        query_grad, key_grad, value_grad = compute()
        return ((totals[0] + key_grad, totals[1] + value_grad), query_grad)

    zero_start = jnp.zeros((key_count, groups, HEAD_SIZE), jnp.float32)
    grad_inputs = (query_blocks, grad_blocks, place_blocks, doc_blocks, log_blocks, delta_blocks)
    (key_total, value_total), query_parts = lax.scan(
        block_grad, (zero_start, zero_start), grad_inputs
    )
    q_summed = lax.psum_scatter(
        query_parts.reshape(query_total, pair_heads, group_width).astype(jnp.bfloat16),
        "dp",
        scatter_dimension=0,
        tiled=True,
    )
    spread_key, spread_value = (
        lax.all_to_all(
            key_total.reshape(key_count, group_width).astype(jnp.bfloat16),
            "head",
            split_axis=0,
            concat_axis=1,
            tiled=True,
        ).astype(jnp.float32),
        lax.all_to_all(
            value_total.reshape(key_count, group_width).astype(jnp.bfloat16),
            "head",
            split_axis=0,
            concat_axis=1,
            tiled=True,
        ).astype(jnp.float32),
    )
    k_summed, v_summed = (
        lax.psum_scatter(
            spread_key.astype(jnp.bfloat16), "srv", scatter_dimension=0, tiled=True
        ).astype(jnp.float32),
        lax.psum_scatter(
            spread_value.astype(jnp.bfloat16), "srv", scatter_dimension=0, tiled=True
        ).astype(jnp.float32),
    )
    return (attention, q_summed, k_summed.astype(jnp.bfloat16), v_summed.astype(jnp.bfloat16))


def solution(mesh):
    placed = (
        P("dp", "srv", "head"),
        P(("dp", "head"), None),
        P(("dp", "head"), None),
        P("dp", "srv", "head"),
        P("dp"),
    )
    return jax.shard_map(
        local,
        mesh=mesh,
        in_specs=placed,
        out_specs=(
            P("dp", "srv", "head"),
            P("dp", "srv", "head"),
            P(("dp", "head", "srv"), None),
            P(("dp", "head", "srv"), None),
        ),
        check_vma=False,
    )
```

profile of v0, /device:TPU:2, one launch (start us, length us, event | category | flops | bytes accessed | tf_op | source)
XLA Modules:
  0.0 651.0 jit_solution(6897663471784736279)
XLA Ops:
  9.5 9.2 %all-to-all-start = ((bf16[80,8,128]{2,0,1:T(8,128)(2,1)}), bf16[80,8,128]{2,0,1:T(8,128)(2,1)S(1)}, u32[]{:S(2)}, u32[]{:S(2)}) async-start(bf16[80,8,128]{2,0,1:T(8,128)(2,1)} %copy_bitcast_fusion.3), calls=%async_computation | async-start | bytes 327680 | tf_op jit(solution)/shard_map/all_to_all | solution.py:16
  21.0 31.2 %all-gather.1 = s32[16,1,640]{2,1,0:T(1,128)S(1)} all-gather(s32[1,1,640]{2,1,0:T(1,128)S(1)} %reshape.364), channel_id=1, replica_groups=mesh['dp'=16,'head'=8,'srv'=4] {'dp'}, dimensions={0}, use_global_device_ids=true | all-gather | bytes 43520 | tf_op jit(solution)/shard_map/all_gather | solution.py:23
  52.8 33.4 %all-gather.5.cloned.1.call-done = bf16[2048,2,128]{2,0,1:T(8,128)(2,1)} async-done(((bf16[128,2,128]{2,0,1:T(8,128)(2,1)}), bf16[2048,2,128]{2,0,1:T(8,128)(2,1)}) %all-gather.5.cloned.1.call-update) | async-done | bytes 1048592 | tf_op jit(solution)/shard_map/all_gather | solution.py:29
  87.6 4.8 all-to-all-start.1
  92.4 7.6 %while.39 = (s32[]{:T(128)}, f32[4,512,2,1]{1,0,2,3:T(4,128)S(1)}, s32[4,512]{1,0:T(4,128)}, s32[640]{0:T(1024)S(1)}, s32[4,512]{1,0:T(4,128)S(1)}, /*index=5*/b...) while((s32[]{:T(128)}, f32[4,512,2,1]{1,0,2,3:T(4,128)S(1)}, ...), condition=%wide.region_2.3_spmd.clone, body=%wide.region_0.2_spmd.clone.sunk | while | flops 170720896 | bytes 1121917 | solution.py:64
  100.0 55.1 %pmax.7 = f32[2048,2,1]{0,1,2:T(2,128)} all-reduce(f32[2048,2,1]{0,1,2:T(2,128)S(1)} %reshape.354), channel_id=1, replica_groups=mesh['dp'=16,'head'=8,'srv'=4] {'dp'}, use_global_device_ids=true, to_apply=%region_3.4 | all-reduce | flops 4096 | bytes 32768 | tf_op jit(solution)/shard_map/pmax | solution.py:65
  155.1 22.3 %while.40 = (s32[]{:T(128)}, f32[4,512,2,128]{3,2,1,0:T(2,128)S(1)}, f32[4,512,2,1]{1,3,2,0:T(1,128)}, s32[4,512]{1,0:T(4,128)}, s32[640]{0:T(1024)S(1)}, /*inde...) while((s32[]{:T(128)}, ...), condition=%wide.region_6.7_spmd.clone, body=%wide.region_4.6_spmd.clone.sunk | while | flops 341769856 | bytes 8437397 | solution.py:89
  183.0 63.6 %reduce-scatter.8.cloned.1.call-done = f32[128,2]{1,0:T(8,128)} async-done(((f32[2048,2]{1,0:T(8,128)}), f32[128,2]{1,0:T(8,128)}) %reduce-scatter.8.cloned.1.call-update) | async-done | bytes 1040
  248.3 27.4 %all_gather.17 = f32[2048,2,1]{0,1,2:T(2,128)S(1)} all-gather(f32[128,2,1]{0,1,2:T(2,128)S(1)} %log_add_fusion), channel_id=1, replica_groups=mesh['dp'=16,'head'=8,'srv'=4] {'dp'}, dimensions={0}, use_global_device_ids=true | all-gather | bytes 17408 | tf_op jit(solution)/shard_map/all_gather | solution.py:106
  275.7 115.2 %all-reduce.10.cloned.1.call-done = f32[2048,2,128]{2,1,0:T(2,128)} async-done(((f32[2048,2,128]{2,1,0:T(2,128)}), f32[2048,2,128]{2,1,0:T(2,128)}) %all-reduce.10.cloned.1.call-update) | async-done | bytes 2097168
  392.6 35.8 %all-gather = f32[2048,2]{1,0:T(8,128)S(1)} all-gather(f32[128,2]{1,0:T(8,128)S(1)} %get-tuple-element.445), channel_id=2, replica_groups=mesh['dp'=16,'head'=8,'srv'=4] {'dp'}, dimensions={0}, use_global_device_ids=true | all-gather | bytes 17408 | tf_op jit(solution)/shard_map/all_gather | solution.py:107
  428.7 32.1 %all-gather.7.cloned.1.call-done = bf16[2048,2,128]{2,0,1:T(8,128)(2,1)} async-done(((bf16[128,2,128]{2,0,1:T(8,128)(2,1)}), bf16[2048,2,128]{2,0,1:T(8,128)(2,1)}) %all-gather.7.cloned.1.call-update) | async-done | bytes 1048592 | tf_op jit(solution)/shard_map/all_gather | solution.py:30
  460.8 37.4 %while.41 = (s32[]{:T(128)}, f32[640,1,128]{0,2,1:T(8,128)S(1)}, f32[640,1,128]{0,2,1:T(8,128)}, bf16[4,512,2,128]{3,1,2,0:T(8,128)(2,1)}, bf16[4,512,2,1,128]{4...) while((s32[]{:T(128)}, f32[640,1,128]{0,2,1:T(8,128)S(1)}, ...), condition=%wide.region_11.12_spmd.clone, body=%wide.region_10.11_spmd.clone.sunk | while | flops 846938752 | bytes 35077916 | solution.py:151
  465.0 3.6 fusion.122
  474.4 3.6 fusion.122
  483.7 3.6 fusion.122
  493.1 3.6 fusion.122
  499.0 4.9 all-to-all-start.2
  503.9 3.3 copy.77
  508.9 4.8 all-to-all-start.3
  513.7 5.0 all-to-all-done.3
  518.8 12.6 %fusion.72 = (bf16[24,1024]{1,0:T(8,128)(2,1)S(1)}, bf16[24,1024]{1,0:T(8,128)(2,1)S(1)}) fusion(bf16[80,1024]{1,0:T(8,128)(2,1)S(1)} %copy_bitcast_fusion.1, bf16[80,1024]{1,0:T(8,128)(2,1)S(1)} %copy_bitcast_fusion), kind=kCustom, calls=%all-reduce-scatter.2 | all-reduce-scatter fusion | flops 196609 | bytes 428032
  533.0 3.1 collective-permute-start.1
  539.6 103.4 %all-reduce.12.cloned.1.call-done = bf16[2048,2,128]{2,1,0:T(2,128)(2,1)} async-done(((bf16[2048,2,128]{2,1,0:T(2,128)(2,1)}), bf16[2048,2,128]{2,1,0:T(2,128)(2,1)}) %all-reduce.12.cloned.1.call-update) | async-done | bytes 1048592
  (173 shorter events, 76.1 us)
Async XLA Ops:
  7.2 1.6 copy-start
  7.2 85.2 %copy-start.3 = (s32[640]{0:T(1024)S(1)}, s32[640]{0:T(1024)}, u32[]{:S(2)}) copy-start(s32[640]{0:T(1024)} %param.15) | copy-start | bytes 7684
  7.2 79.1 %all-gather.5.cloned.1.call-start = ((), (), s32[]{:S(2)}) async-start(), calls=%async_computation.5 | async-start | bytes 1114112 | tf_op jit(solution)/shard_map/all_gather | solution.py:29
  9.5 78.1 %all-to-all-start = ((bf16[80,8,128]{2,0,1:T(8,128)(2,1)}), bf16[80,8,128]{2,0,1:T(8,128)(2,1)S(1)}, u32[]{:S(2)}, u32[]{:S(2)}) async-start(bf16[80,8,128]{2,0,1:T(8,128)(2,1)} %copy_bitcast_fusion.3), calls=%async_computation | async-start | bytes 327680 | tf_op jit(solution)/shard_map/all_to_all | solution.py:16
  87.6 67.6 %all-to-all-start.1 = ((bf16[80,8,128]{2,0,1:T(8,128)(2,1)}), bf16[80,8,128]{2,0,1:T(8,128)(2,1)}, u32[]{:S(2)}, u32[]{:S(2)}) async-start(bf16[80,8,128]{2,0,1:T(8,128)(2,1)} %copy_bitcast_fusion.2), calls=%async_computation.1 | async-start | bytes 327680 | tf_op jit(solution)/shard_map/all_to_all | solution.py:17
  92.4 154.2 %reduce-scatter.8.cloned.1.call-start = ((), (), s32[]{:S(2)}) async-start(), calls=%async_computation.7 | async-start | bytes 1114112
  177.4 2.2 copy-start.2
  177.4 2.9 copy-start.7
  179.6 211.3 %all-reduce.10.cloned.1.call-start = ((), (), s32[]{:S(2)}) async-start(), calls=%async_computation.8 | async-start | bytes 4194304
  180.3 280.5 %all-gather.7.cloned.1.call-start = ((), (), s32[]{:S(2)}) async-start(), calls=%async_computation.6 | async-start | bytes 1114112 | tf_op jit(solution)/shard_map/all_gather | solution.py:30
  461.3 3.2 copy-start.1
  465.0 3.6 copy-start.4
  470.7 3.2 copy-start.1
  474.4 3.6 copy-start.4
  480.0 3.2 copy-start.1
  483.7 3.6 copy-start.4
  489.4 3.2 copy-start.1
  493.1 3.6 copy-start.4
  498.2 9.0 %copy-start.6 = (f32[640,1,128]{0,2,1:T(8,128)S(1)}, f32[640,1,128]{0,2,1:T(8,128)}, u32[]{:S(2)}) copy-start(f32[640,1,128]{0,2,1:T(8,128)} %get-tuple-element.183) | copy-start | bytes 983044
  499.0 9.9 %all-to-all-start.2 = ((bf16[8,80,128]{2,1,0:T(8,128)(2,1)}), bf16[8,80,128]{2,1,0:T(8,128)(2,1)S(1)}, u32[]{:S(2)}, u32[]{:S(2)}) async-start(bf16[8,80,128]{2,1,0:T(8,128)(2,1)} %bitcast.15), calls=%async_computation.2 | async-start | bytes 327680 | tf_op jit(solution)/shard_map/all_to_all | solution.py:161
  503.9 139.1 %all-reduce.12.cloned.1.call-start = ((), (), s32[]{:S(2)}) async-start(), calls=%async_computation.9 | async-start | bytes 2097152
  508.9 9.8 %all-to-all-start.3 = ((bf16[8,80,128]{2,1,0:T(8,128)(2,1)}), bf16[8,80,128]{2,1,0:T(8,128)(2,1)S(1)}, u32[]{:S(2)}, u32[]{:S(2)}) async-start(bf16[8,80,128]{2,1,0:T(8,128)(2,1)} %bitcast.17), calls=%async_computation.3 | async-start | bytes 327680 | tf_op jit(solution)/shard_map/all_to_all | solution.py:168
  531.4 6.6 %collective-permute-start = (bf16[12,1024]{1,0:T(8,128)(2,1)S(1)}, bf16[12,1024]{1,0:T(8,128)(2,1)S(1)}, u32[]{:S(2)}, u32[]{:S(2)}) collective-permute-start(bf16[12,1024]{1,0:T(8,128)(2,1)S(1)} %slice.16), channel_id=1, source_target_pairs={{0,1},{1,2},{2,3},{4,5},{5,6},{6,7},{8,9},{9,10},{10,11},{12,13},{... | collective-permute-start | bytes 73736
  533.0 5.2 collective-permute-start.1
  (4 other events, 4.0 us)
Sparse Core Ops, SparseCore 0:
  10.7 75.5 all-gather.4
  179.7 66.8 reduce-scatter.7
  249.1 141.7 all-reduce.9
  393.6 67.1 all-gather.6
  507.3 135.5 all-reduce.11
where the time goes:
time: 653 us; the launch traced here: 651 us
  waiting for transfers between devices  354 us (54%)
  blocking collectives  162 us (25%)
  matrix products  42.8 us (7%)
  local copies, waits for them, and re-layouts  40.5 us (6%)
  starting transfers between devices  28.4 us (4%)
  between operations  15.3 us (2%)
  other arithmetic  7 us (1%)
    unnamed x10, waiting for transfers between devices  283 us
    pmax x1, blocking collectives, local(): row_max = lax.pmax(local_max.reshape(query_total, pair_heads, groups), 'dp')  55.1 us
    all_gather x1, blocking collectives, local(): lax.all_gather(delta_home, 'dp', axis=0, tiled=True)  35.8 us
    all_gather x1, waiting for transfers between devices, local(): lax.all_gather(queries, 'dp', axis=0, tiled=True)  33.4 us
    all_gather x1, waiting for transfers between devices, local(): lax.all_gather(output_gradient, 'dp', axis=0, tiled=True)  32.1 us
    all_gather x1, blocking collectives, local(): all_docs = lax.all_gather(doc_ids, 'dp', axis=0, tiled=True)  31.2 us
    all_gather x1, blocking collectives, local(): lax.all_gather(log_home, 'dp', axis=0, tiled=True)  27.4 us
    dot_general x4, matrix products, compute(): jnp.einsum('gjpk,pjgd->kgd', probs.astype(jnp.bfloat16), grad_block, pref...  14.3 us
  transfers between devices with their start and end apart: 11, of which 7 were waited for; matrix products, arithmetic and copies ran while one was open for 6% of the time, Pallas kernels for 0%

commit v1 on v0

--- a/solution.py
+++ b/solution.py
@@ -25,9 +25,13 @@
     context = all_docs.shape[0] - query_total
     query_docs = all_docs[context:]
     query_places = context + jnp.arange(query_total, dtype=jnp.int32)
+    plan_pairs_all = lambda block_here, dim_no: jnp.concatenate(
+        lax.all_to_all(jnp.stack([block_here for _ in range(lax.axis_size("dp"))], 0), "dp", 0, 0),
+        dim_no,
+    )
     all_q, all_dout = (
         lax.all_gather(queries, "dp", axis=0, tiled=True),
-        lax.all_gather(output_gradient, "dp", axis=0, tiled=True),
+        plan_pairs_all(output_gradient, dim_no=0),
     )
     block_rows = math.gcd(512, query_total)
     block_count = query_total // block_rows

time: 653 us -> 618 us (0.946)
  waiting for transfers between devices: 354 us -> 323 us
    all_gather x1 -> x0, waiting for transfers between devices: 32.1 us -> none  [local(): lax.all_gather(output_gradient, 'dp', axis=0, tiled=True)]
    dynamic_slice x12, local copies, waits for them, and re-layouts: 8.69 us -> 0.12 us  [local(): local_max = lax.map(block_top, (query_blocks, place_blocks, doc_blocks))]
    unnamed x10 -> x9, waiting for transfers between devices: 283 us -> 284 us
    unnamed x26 -> x24, local copies, waits for them, and re-layouts: 13.2 us -> 12.7 us
  transfers between devices with their start and end apart: 11 -> 11, of which waited for: 7 -> 6; matrix products, arithmetic and copies ran while one was open for 6% -> 8% of each run, Pallas kernels for 0% -> 0%
where the time goes in v1:
time: 618 us; the launch traced here: 617 us
  waiting for transfers between devices  323 us (52%)
  blocking collectives  166 us (27%)
  matrix products  39.1 us (6%)
  local copies, waits for them, and re-layouts  34.3 us (6%)
  starting transfers between devices  32.2 us (5%)
  between operations  15.3 us (2%)
    unnamed x9, waiting for transfers between devices  284 us
    pmax x1, blocking collectives, local(): row_max = lax.pmax(local_max.reshape(query_total, pair_heads, groups), 'dp')  58 us
    all_gather x1, blocking collectives, local(): lax.all_gather(delta_home, 'dp', axis=0, tiled=True)  34.5 us
    all_gather x1, waiting for transfers between devices, local(): lax.all_gather(queries, 'dp', axis=0, tiled=True)  33.2 us
    all_gather x1, blocking collectives, local(): all_docs = lax.all_gather(doc_ids, 'dp', axis=0, tiled=True)  31.2 us
    all_gather x1, blocking collectives, local(): lax.all_gather(log_home, 'dp', axis=0, tiled=True)  29.7 us
    dot_general x4, matrix products, compute(): jnp.einsum('gjpk,pjgd->kgd', probs.astype(jnp.bfloat16), grad_block, pref...  14.2 us
    unnamed x1, blocking collectives  12.8 us
  transfers between devices with their start and end apart: 11, of which 6 were waited for; matrix products, arithmetic and copies ran while one was open for 8% of the time, Pallas kernels for 0%

profile of v1, /device:TPU:2, one launch (start us, length us, event | category | flops | bytes accessed | tf_op | source)
XLA Modules:
  0.0 616.9 jit_solution(4216063106920843114)
XLA Ops:
  9.5 9.2 %all-to-all-start = ((bf16[80,8,128]{2,0,1:T(8,128)(2,1)}), bf16[80,8,128]{2,0,1:T(8,128)(2,1)S(1)}, u32[]{:S(2)}, u32[]{:S(2)}) async-start(bf16[80,8,128]{2,0,1:T(8,128)(2,1)} %copy_bitcast_fusion.3), calls=%async_computation | async-start | bytes 327680 | tf_op jit(solution)/shard_map/all_to_all | solution.py:16
  21.0 31.2 %all-gather.1 = s32[16,1,640]{2,1,0:T(1,128)S(1)} all-gather(s32[1,1,640]{2,1,0:T(1,128)S(1)} %reshape.362), channel_id=1, replica_groups=mesh['dp'=16,'head'=8,'srv'=4] {'dp'}, dimensions={0}, use_global_device_ids=true | all-gather | bytes 43520 | tf_op jit(solution)/shard_map/all_gather | solution.py:23
  53.1 33.2 %all-gather.4.cloned.1.call-done = bf16[2048,2,128]{2,0,1:T(8,128)(2,1)} async-done(((bf16[128,2,128]{2,0,1:T(8,128)(2,1)}), bf16[2048,2,128]{2,0,1:T(8,128)(2,1)}) %all-gather.4.cloned.1.call-update) | async-done | bytes 1048592 | tf_op jit(solution)/shard_map/all_gather | solution.py:33
  87.6 4.8 all-to-all-start.1
  92.4 4.8 while.39
  97.2 58.0 %pmax.7 = f32[2048,2,1]{0,1,2:T(2,128)S(1)} all-reduce(f32[2048,2,1]{0,1,2:T(2,128)S(1)} %reshape.353), channel_id=1, replica_groups=mesh['dp'=16,'head'=8,'srv'=4] {'dp'}, use_global_device_ids=true, to_apply=%region_3.4 | all-reduce | flops 4096 | bytes 32768 | tf_op jit(solution)/shard_map/pmax | solution.py:69
  156.4 3.9 all-to-all-start.2
  160.4 14.1 %while.40 = (s32[]{:T(128)}, f32[4,512,2,128]{3,2,1,0:T(2,128)}, f32[4,512,2,1]{1,3,2,0:T(1,128)S(1)}, s32[4,512]{1,0:T(4,128)S(1)}, s32[640]{0:T(1024)S(1)}, /*...) while((s32[]{:T(128)}, f32[4,512,2,128]{3,2,1,0:T(2,128)}, ...), condition=%wide.region_6.7_spmd.clone, body=%wide.region_4.6_spmd.clone.sunk | while | flops 341769856 | bytes 8437397 | solution.py:93
  178.6 68.9 %reduce-scatter.8.cloned.1.call-done = f32[128,2]{1,0:T(8,128)} async-done(((f32[2048,2]{1,0:T(8,128)}), f32[128,2]{1,0:T(8,128)}) %reduce-scatter.8.cloned.1.call-update) | async-done | bytes 1040
  248.6 29.7 %all_gather.14 = f32[2048,2,1]{0,1,2:T(2,128)} all-gather(f32[128,2,1]{0,1,2:T(2,128)S(1)} %log_add_fusion), channel_id=1, replica_groups=mesh['dp'=16,'head'=8,'srv'=4] {'dp'}, dimensions={0}, use_global_device_ids=true | all-gather | bytes 17408 | tf_op jit(solution)/shard_map/all_gather | solution.py:110
  279.3 112.7 %all-reduce.10.cloned.1.call-done = f32[2048,2,128]{2,1,0:T(2,128)} async-done(((f32[2048,2,128]{2,1,0:T(2,128)}), f32[2048,2,128]{2,1,0:T(2,128)}) %all-reduce.10.cloned.1.call-update) | async-done | bytes 2097168
  393.7 34.5 %all-gather = f32[2048,2]{1,0:T(8,128)S(1)} all-gather(f32[128,2]{1,0:T(8,128)S(1)} %get-tuple-element.445), channel_id=2, replica_groups=mesh['dp'=16,'head'=8,'srv'=4] {'dp'}, dimensions={0}, use_global_device_ids=true | all-gather | bytes 17408 | tf_op jit(solution)/shard_map/all_gather | solution.py:111
  428.6 36.8 %while.41 = (s32[]{:T(128)}, f32[640,1,128]{0,2,1:T(8,128)S(1)}, f32[640,1,128]{0,2,1:T(8,128)}, bf16[4,512,2,128]{3,1,2,0:T(8,128)(2,1)}, bf16[4,512,2,1,128]{4...) while((s32[]{:T(128)}, f32[640,1,128]{0,2,1:T(8,128)S(1)}, ...), condition=%wide.region_11.12_spmd.clone, body=%wide.region_10.11_spmd.clone.sunk | while | flops 846938752 | bytes 35077916 | solution.py:155
  432.6 3.5 fusion.122
  441.8 3.6 fusion.122
  451.0 3.6 fusion.122
  460.2 3.6 fusion.122
  466.1 4.6 all-to-all-start.3
  470.8 3.3 copy.78
  475.8 4.8 all-to-all-start.4
  480.5 5.0 all-to-all-done.4
  485.6 12.8 %fusion.72 = (bf16[24,1024]{1,0:T(8,128)(2,1)S(1)}, bf16[24,1024]{1,0:T(8,128)(2,1)S(1)}) fusion(bf16[80,1024]{1,0:T(8,128)(2,1)S(1)} %copy_bitcast_fusion.1, bf16[80,1024]{1,0:T(8,128)(2,1)S(1)} %copy_bitcast_fusion), kind=kCustom, calls=%all-reduce-scatter.2 | all-reduce-scatter fusion | flops 196609 | bytes 428032
  499.8 3.4 collective-permute-start.1
  506.8 102.0 %all-reduce.12.cloned.1.call-done = bf16[2048,2,128]{2,1,0:T(2,128)(2,1)} async-done(((bf16[2048,2,128]{2,1,0:T(2,128)(2,1)}), bf16[2048,2,128]{2,1,0:T(2,128)(2,1)}) %all-reduce.12.cloned.1.call-update) | async-done | bytes 1048592
  (172 shorter events, 64.7 us)
Async XLA Ops:
  7.2 1.6 copy-start
  7.2 85.2 %copy-start.2 = (s32[640]{0:T(1024)S(1)}, s32[640]{0:T(1024)}, u32[]{:S(2)}) copy-start(s32[640]{0:T(1024)} %param.15) | copy-start | bytes 7684
  7.2 79.1 %all-gather.4.cloned.1.call-start = ((), (), s32[]{:S(2)}) async-start(), calls=%async_computation.6 | async-start | bytes 1114112 | tf_op jit(solution)/shard_map/all_gather | solution.py:33
  9.5 78.1 %all-to-all-start = ((bf16[80,8,128]{2,0,1:T(8,128)(2,1)}), bf16[80,8,128]{2,0,1:T(8,128)(2,1)S(1)}, u32[]{:S(2)}, u32[]{:S(2)}) async-start(bf16[80,8,128]{2,0,1:T(8,128)(2,1)} %copy_bitcast_fusion.3), calls=%async_computation | async-start | bytes 327680 | tf_op jit(solution)/shard_map/all_to_all | solution.py:16
  87.6 67.7 %all-to-all-start.1 = ((bf16[80,8,128]{2,0,1:T(8,128)(2,1)}), bf16[80,8,128]{2,0,1:T(8,128)(2,1)S(1)}, u32[]{:S(2)}, u32[]{:S(2)}) async-start(bf16[80,8,128]{2,0,1:T(8,128)(2,1)} %copy_bitcast_fusion.2), calls=%async_computation.1 | async-start | bytes 327680 | tf_op jit(solution)/shard_map/all_to_all | solution.py:17
  156.4 121.8 %all-to-all-start.2 = ((bf16[16,128,2,128]{3,1,2,0:T(8,128)(2,1)}), bf16[16,128,2,128]{3,1,2,0:T(8,128)(2,1)S(1)}, u32[]{:S(2)}, u32[]{:S(2)}) async-start(bf16[16,128,2,128]{3,1,2,0:T(8,128)(2,1)} %stack.2), calls=%async_computation.2 | async-start | bytes 2097152 | tf_op jit(solution)/shard_map/all_to_all | solution.py:29
  160.4 87.1 %reduce-scatter.8.cloned.1.call-start = ((), (), s32[]{:S(2)}) async-start(), calls=%async_computation.7 | async-start | bytes 1114112
  175.9 216.1 %copy-start.6 = (bf16[128,2,128]{2,1,0:T(2,128)(2,1)S(1)}, bf16[128,2,128]{2,1,0:T(2,128)(2,1)}, u32[]{:S(2)}) copy-start(bf16[128,2,128]{2,1,0:T(2,128)(2,1)} %param.14) | copy-start | bytes 196612
  175.9 216.1 %all-reduce.10.cloned.1.call-start = ((), (), s32[]{:S(2)}) async-start(), calls=%async_computation.8 | async-start | bytes 4194304
  429.1 3.0 copy-start.1
  432.6 3.5 copy-start.3
  436.7 1.0 copy-start.4
  438.3 3.0 copy-start.1
  441.8 3.6 copy-start.3
  447.5 3.0 copy-start.1
  451.0 3.6 copy-start.3
  456.6 3.0 copy-start.1
  460.2 3.6 copy-start.3
  465.3 8.7 %copy-start.5 = (f32[640,1,128]{0,2,1:T(8,128)S(1)}, f32[640,1,128]{0,2,1:T(8,128)}, u32[]{:S(2)}) copy-start(f32[640,1,128]{0,2,1:T(8,128)} %get-tuple-element.183) | copy-start | bytes 983044
  466.1 9.7 %all-to-all-start.3 = ((bf16[8,80,128]{2,1,0:T(8,128)(2,1)}), bf16[8,80,128]{2,1,0:T(8,128)(2,1)S(1)}, u32[]{:S(2)}, u32[]{:S(2)}) async-start(bf16[8,80,128]{2,1,0:T(8,128)(2,1)} %bitcast.15), calls=%async_computation.3 | async-start | bytes 327680 | tf_op jit(solution)/shard_map/all_to_all | solution.py:165
  470.7 138.1 %all-reduce.12.cloned.1.call-start = ((), (), s32[]{:S(2)}) async-start(), calls=%async_computation.9 | async-start | bytes 2097152
  475.8 9.8 %all-to-all-start.4 = ((bf16[8,80,128]{2,1,0:T(8,128)(2,1)}), bf16[8,80,128]{2,1,0:T(8,128)(2,1)S(1)}, u32[]{:S(2)}, u32[]{:S(2)}) async-start(bf16[8,80,128]{2,1,0:T(8,128)(2,1)} %bitcast.17), calls=%async_computation.4 | async-start | bytes 327680 | tf_op jit(solution)/shard_map/all_to_all | solution.py:172
  498.5 6.7 %collective-permute-start = (bf16[12,1024]{1,0:T(8,128)(2,1)S(1)}, bf16[12,1024]{1,0:T(8,128)(2,1)S(1)}, u32[]{:S(2)}, u32[]{:S(2)}) collective-permute-start(bf16[12,1024]{1,0:T(8,128)(2,1)S(1)} %slice.16), channel_id=1, source_target_pairs={{0,1},{1,2},{2,3},{4,5},{5,6},{6,7},{8,9},{9,10},{10,11},{12,13},{... | collective-permute-start | bytes 73736
  499.8 5.5 collective-permute-start.1
  (3 other events, 3.0 us)
Sparse Core Ops, SparseCore 0:
  10.7 75.5 all-gather.3
  176.1 71.4 reduce-scatter.7
  250.0 141.9 all-reduce.9
  474.2 134.5 all-reduce.11
